TPU v7x, 1024 devices: a whole 4x4x32 slice. The times are simulated.
1024 devices in a mesh: domain: 64 (over x, z_lo, core), panel: 16 (over z_hi, y).
Axes of the slice: x: 4, y: 4, z: 32 (z_hi: 4, z_lo: 8; z = z_hi * 8 + z_lo), core: 2. Of those that a mesh axis runs over, the one named last changes fastest.
Arguments:
- eigvec: bfloat16 [98304, 8192], P('domain', 'panel'), may hold values from -0.01953125 to 0.01953125
- flux: bfloat16 [98304, 768], P('domain'), may hold values from -64 to 64
- blocks: int32 [256, 2], P('domain'), may hold values from 0 to 5, as said below
- tile_mask: int32 [16, 2, 4, 4], P('panel'), may hold values 0 or 1
- freq: bfloat16 [16, 512], P('panel'), may hold values from 0.5 to 2
Outputs:
- pair_self: float32 [16, 512, 512], P('panel', 'domain')
- pair_next: float32 [16, 512, 512], P('panel', 'domain')
- diffusivity: float32 [16, 512], P('panel', 'domain')
Inputs may be any that keep to these rules, and one draw needn't show every extreme that they name: Atom block g, which is block g mod 4 of its slab of 4 blocks, lists two different blocks among itself and its two neighbours along the atom order, numbered in its slab extended by one block on each side (so entries lie in g mod 4 to g mod 4 + 2), the order being periodic. The first and the last block of every slab list the two blocks beside them.
All inputs are finite; a program needn't handle non-finite values. No bound on the sum of `tile_mask` on one device may be relied on, other than what follows from the above.
Results may differ from a plain program's by a relative error of at most 0.0029.
Values may be sent and summed in bfloat16 or wider, within the bound.
A program may use at most 32 MiB of HBM per device.

v0:
```python
import math

import jax
import jax.numpy as jnp
from jax import lax
from jax.sharding import PartitionSpec as P

BLK = 128


lorentz_width = 0.25


def padded(cells, sides, width):
    for axis, dim in sides:
        count = lax.axis_size(axis)
        head = lax.slice_in_dim(cells, 0, width, axis=dim)
        tail = lax.slice_in_dim(cells, cells.shape[dim] - width, cells.shape[dim], axis=dim)
        cells = jnp.concatenate(
            [
                lax.ppermute(tail, axis, [(i, (i + 1) % count) for i in range(count)]),
                cells,
                lax.ppermute(head, axis, [((i + 1) % count, i) for i in range(count)]),
            ],
            axis=dim,
        )
    return cells


def shifted(value, axis, steps):
    count = lax.axis_size(axis)
    initial, last = (max(0, -steps), min(count, count - steps))
    return lax.ppermute(value, axis, [(source, source + steps) for source in range(initial, last)])


def lorentz(gap):
    return lorentz_width / math.pi / (gap * gap + lorentz_width * lorentz_width)


def contract(eigvec, right):
    return lax.dot_general(
        eigvec, right, (((0,), (0,)), ((), ())), preferred_element_type=jnp.float32
    )


def shards(eigvec, flux, blocks, tile_mask, freq):
    span = 3 * BLK
    count_blocks = eigvec.shape[0] // span
    modes = eigvec.shape[1]
    neighbours = blocks.shape[1]
    extended = padded(eigvec, (("domain", 0),), span)
    stacked = extended.reshape(count_blocks + 2, span, modes)
    picked = jnp.take(stacked, blocks, axis=0).reshape(count_blocks, neighbours * span, modes)
    couplings = flux.reshape(count_blocks, span, neighbours * span)
    image = jnp.einsum("bij,bjm->bim", couplings, picked, preferred_element_type=jnp.float32)
    image = image.astype(jnp.bfloat16).reshape(count_blocks * span, modes)
    keep = modes // lax.axis_size("domain")
    following, freq_next = shifted((image, freq), "panel", -1)
    joined = jnp.concatenate((image, following), axis=1)
    pairs = lax.psum_scatter(contract(eigvec, joined), "domain", scatter_dimension=0, tiled=True)
    own_pairs = pairs[:, :modes]
    next_pairs = pairs[:, modes:]
    start = lax.axis_index("domain") * keep
    grid = tile_mask[0].astype(jnp.float32)
    tile = modes // grid.shape[-1]
    full = jnp.repeat(jnp.repeat(grid, tile, axis=1), tile, axis=2)
    rows_mask = lax.dynamic_slice_in_dim(full, start, keep, 1)
    own_pairs = own_pairs * rows_mask[0]
    next_pairs = next_pairs * rows_mask[1]
    own_freq = freq[0].astype(jnp.float32)
    next_freq = freq_next[0].astype(jnp.float32)
    mine = lax.dynamic_slice_in_dim(own_freq, start, keep, 0)
    weight_own = lorentz(mine[:, None] - own_freq[None, :])
    weight_next = lorentz(mine[:, None] - next_freq[None, :])
    total = jnp.sum(
        own_pairs * own_pairs * weight_own + next_pairs * next_pairs * weight_next, axis=1
    )
    diffusivity = math.pi / 3.0 * total / (2.0 * modes * mine * mine)
    return (own_pairs[None], next_pairs[None], diffusivity[None])


def solution(mesh):
    return jax.shard_map(
        shards,
        mesh=mesh,
        in_specs=(
            P("domain", "panel"),
            P("domain", None),
            P("domain", None),
            P("panel", None, None, None),
            P("panel", None),
        ),
        out_specs=(P("panel", "domain", None), P("panel", "domain", None), P("panel", "domain")),
        check_vma=False,
    )
```

profile of v0, /device:TPU:24, one launch (start us, length us, event | category | flops | bytes accessed | tf_op | source)
XLA Modules:
  0.0 799.0 jit_solution(5933432321972708024)
XLA Ops:
  7.2 2.1 fusion.15
  9.3 1.9 collective-permute-start
  11.2 14.8 %collective-permute-start.1 = (bf16[384,512]{1,0:T(8,128)(2,1)S(1)}, bf16[384,512]{1,0:T(8,128)(2,1)S(1)}, u32[]{:S(2)}, u32[]{:S(2)}) collective-permute-start(bf16[384,512]{1,0:T(8,128)(2,1)S(1)} %get-tuple-element.16), channel_id=1, source_target_pairs={{16,0},{32,16},{48,32},{64,48},{80,64},{96,80},{112,96},{128,112},... | collective-permute-start | bytes 1179656 | tf_op jit(solution)/shard_map/ppermute | solution.py:23
  26.0 0.7 compare_select_fusion
  26.7 0.1 copy.21
  26.8 0.1 reshape.42
  26.9 0.7 compare_and_fusion
  27.6 2.5 collective-permute-done
  30.0 1.2 collective-permute-done.1
  31.3 3.0 pad_maximum_fusion
  34.3 4.1 gather_fusion
  38.4 2.2 bitcast_select_fusion
  40.6 1.4 convolution_convert_fusion
  42.0 2.7 collective-permute-start.2
  44.7 271.9 %collective-permute-done.2 = bf16[1536,512]{1,0:T(8,128)(2,1)S(1)} collective-permute-done((bf16[1536,512]{1,0:T(8,128)(2,1)S(1)}, bf16[1536,512]{1,0:T(8,128)(2,1)S(1)}, u32[]{:S(2)}, u32[]{:S(2)}) %collective-permute-start.2) | collective-permute-done | bytes 1572896 | tf_op jit(solution)/shard_map/ppermute | solution.py:33
  316.6 3.1 fusion.4
  319.7 3.0 copy.24
  322.7 1.9 collective-permute-start.3
  324.8 2.2 broadcast_in_dim.41
  327.0 3.1 reshape.37
  330.1 8.9 %collective-permute-done.3 = bf16[1,512]{1,0:T(2,128)(2,1)S(1)} collective-permute-done((bf16[1,512]{1,0:T(2,128)(2,1)S(1)}, bf16[1,512]{1,0:T(2,128)(2,1)S(1)}, u32[]{:S(2)}, u32[]{:S(2)}) %collective-permute-start.3) | collective-permute-done | bytes 1056 | tf_op jit(solution)/shard_map/ppermute | solution.py:33
  339.0 451.1 %reduce-scatter.4.cloned.1.call-done = f32[8,1024]{1,0:T(8,128)} async-done(((f32[512,1024]{1,0:T(8,128)}), f32[8,1024]{1,0:T(8,128)}) %reduce-scatter.4.cloned.1.call-update) | async-done | bytes 32784 | tf_op jit(solution)/shard_map/reduce_scatter | solution.py:60
  790.1 1.5 add_reduce_fusion
  791.6 0.6 fusion.13
  (17 shorter events, 0.3 us)
Async XLA Ops:
  7.2 33.5 %copy-start = (bf16[1536,768]{1,0:T(8,128)(2,1)S(1)}, bf16[1536,768]{1,0:T(8,128)(2,1)}, u32[]{:S(2)}) copy-start(bf16[1536,768]{1,0:T(8,128)(2,1)} %param.6) | copy-start | bytes 7077892
  7.2 782.9 %reduce-scatter.4.cloned.1.call-start = ((), (), s32[]{:S(2)}) async-start(), calls=%async_computation.1 | async-start | bytes 2129920 | tf_op jit(solution)/shard_map/reduce_scatter | solution.py:60
  9.3 20.8 %collective-permute-start = (bf16[384,512]{1,0:T(8,128)(2,1)}, bf16[384,512]{1,0:T(8,128)(2,1)S(1)}, u32[]{:S(2)}, u32[]{:S(2)}) collective-permute-start(bf16[384,512]{1,0:T(8,128)(2,1)} %get-tuple-element.15), channel_id=1, source_target_pairs={{0,16},{16,32},{32,48},{48,64},{64,80},{80,96},{96,112},{112,128},... | collective-permute-start | bytes 1179656 | tf_op jit(solution)/shard_map/ppermute | solution.py:21
  11.2 20.1 %collective-permute-start.1 = (bf16[384,512]{1,0:T(8,128)(2,1)S(1)}, bf16[384,512]{1,0:T(8,128)(2,1)S(1)}, u32[]{:S(2)}, u32[]{:S(2)}) collective-permute-start(bf16[384,512]{1,0:T(8,128)(2,1)S(1)} %get-tuple-element.16), channel_id=1, source_target_pairs={{16,0},{32,16},{48,32},{64,48},{80,64},{96,80},{112,96},{128,112},... | collective-permute-start | bytes 1179656 | tf_op jit(solution)/shard_map/ppermute | solution.py:23
  40.6 275.9 %copy-start.1 = (bf16[1536,512]{1,0:T(8,128)(2,1)S(1)}, bf16[1536,512]{1,0:T(8,128)(2,1)}, u32[]{:S(2)}) copy-start(bf16[1536,512]{1,0:T(8,128)(2,1)} %param.5) | copy-start | bytes 4718596
  42.0 274.5 %collective-permute-start.2 = (bf16[1536,512]{1,0:T(8,128)(2,1)S(1)}, bf16[1536,512]{1,0:T(8,128)(2,1)S(1)}, u32[]{:S(2)}, u32[]{:S(2)}) collective-permute-start(bf16[1536,512]{1,0:T(8,128)(2,1)S(1)} %bitcast.53), channel_id=1, source_target_pairs={{1,0},{2,1},{3,2},{4,3},{5,4},{6,5},{7,6},{8,7},{9,8},{10,9},{11,1... | collective-permute-start | bytes 4718600 | tf_op jit(solution)/shard_map/ppermute | solution.py:33
  319.7 3.0 copy-start.3
  319.7 5.0 copy-start.2
  322.7 16.3 %collective-permute-start.3 = (bf16[1,512]{1,0:T(2,128)(2,1)S(1)}, bf16[1,512]{1,0:T(2,128)(2,1)S(1)}, u32[]{:S(2)}, u32[]{:S(2)}) collective-permute-start(bf16[1,512]{1,0:T(2,128)(2,1)S(1)} %copy-done.3), channel_id=1, source_target_pairs={{1,0},{2,1},{3,2},{4,3},{5,4},{6,5},{7,6},{8,7},{9,8},{10,9},{11,1... | collective-permute-start | bytes 3080 | tf_op jit(solution)/shard_map/ppermute | solution.py:33
Sparse Core Ops, SparseCore 0:
  322.8 467.2 reduce-scatter.3
where the time goes:
time: 800 us; the launch traced here: 799 us
  waiting for transfers between devices  736 us (92%)
  starting transfers between devices  21.3 us (3%)
  local copies, waits for them, and re-layouts  14.8 us (2%)
  between operations  14.2 us (2%)
  other arithmetic  8.68 us (1%)
    reduce_scatter x1, waiting for transfers between devices, shards(): lax.psum_scatter(contract(eigvec, joined), 'domain', scatter_dimension=0,...  451 us
    ppermute x2, waiting for transfers between devices, shifted(): lax.ppermute(value, axis, [(source, source + steps) for source in range(i...  281 us
  transfers between devices with their start and end apart: 5, of which 5 were waited for; matrix products, arithmetic and copies ran while one was open for 1% of the time, Pallas kernels for 0%

commit v1 on v0

v1 whole, which is shorter than its diff:
```python
import functools
import math

import jax
import jax.numpy as jnp
from jax import lax
from jax.experimental import pallas as pl
from jax.experimental.pallas import tpu as pltpu
from jax.sharding import PartitionSpec as P

MESH = pl.DeviceIdType.MESH
F32 = jnp.float32
BF16 = jnp.bfloat16

WIDTH = 0.25
SPAN = 384
MODES = 512
PART = 192
SELF, NEXT, PREV = 0, 1, 2
UP_ROWS = (0, 192, 1152, 1344)


def lorentz(gap):
    return WIDTH / math.pi / (gap * gap + WIDTH * WIDTH)


def mm(a, b):
    return jnp.dot(a, b, preferred_element_type=F32)


def mtm(a, b):
    return lax.dot_general(a, b, (((0,), (0,)), ((), ())), preferred_element_type=F32)


def kernel(
    e_ref, f_ref, blocks_ref, mask_ref, freq_ref,
    self_ref, next_ref, diff_ref,
    y_ref, halo, eprev, ynext, relay_up, relay_down,
    freq_mine, freq_next, pairs, core_in, x_out, x_in, z_out, z_in, prev_out, prev_in,
    halo_s, halo_r, up_s, up_r, down_s, down_r, relay_s, relay_r,
    freq_sem, core_sem, x_s, x_r, z_s, z_r, prev_sem,
):
    d = lax.axis_index("domain")
    p = lax.axis_index("panel")
    x, zl, c = d // 16, lax.rem(d // 2, 8), lax.rem(d, 2)
    y, zh = lax.rem(p, 4), p // 4
    has_next, has_prev = p < 15, p > 0
    rises, falls = zh < 3, zh > 0
    after, before = lax.rem(d + 1, 64), lax.rem(d + 63, 64)
    above, below = (d, zh * 4 + 4), (d, zh * 4 - 1)

    def at_x(k):
        return (lax.rem(x + k, 4) * 16 + zl * 2 + c, p)

    def at_z(k):
        return (x * 16 + lax.rem(zl + k, 8) * 2 + c, p)

    def at_y(q):
        return (d, zh * 4 + q)

    def send(src, dst, send_sem, recv_sem, device):
        return pltpu.make_async_remote_copy(
            src_ref=src, dst_ref=dst, send_sem=send_sem, recv_sem=recv_sem,
            device_id=device, device_id_type=MESH,
        )

    barrier = pltpu.get_barrier_semaphore()

    def greet(device):
        pl.semaphore_signal(barrier, inc=1, device_id=device, device_id_type=MESH)

    greet((after, p))
    greet((before, p))
    for k in (1, 2, 3):
        greet(at_y(lax.rem(y + k, 4)))
        greet(at_x(k))
    for k in range(1, 8):
        greet(at_z(k))

    @pl.when((y == 0) & falls)
    def _():
        for q in range(4):
            greet((d, zh * 4 - 4 + q))

    @pl.when((y == 3) & rises)
    def _():
        for q in range(4):
            greet((d, zh * 4 + 4 + q))

    def coupling(g, entry):
        rows = slice(g * SPAN, (g + 1) * SPAN)
        total = None
        for k in range(2):
            listed = jnp.full((1, SPAN), blocks_ref[g, k], jnp.int32) == entry
            weight = jnp.where(listed, 1.0, 0.0).astype(BF16)
            part = f_ref[rows, k * SPAN:(k + 1) * SPAN] * weight
            total = part if total is None else total + part
        return total

    def own_block(b):
        return e_ref[b * SPAN:(b + 1) * SPAN, :]

    for g in (1, 2):
        total = mm(coupling(g, g), own_block(g - 1))
        total += mm(coupling(g, g + 1), own_block(g))
        total += mm(coupling(g, g + 2), own_block(g + 1))
        y_ref[g * SPAN:(g + 1) * SPAN, :] = total.astype(BF16)

    w_row = freq_ref[...].astype(F32)
    freq_mine[...] = jnp.broadcast_to(w_row, (8, MODES))

    pl.semaphore_wait(barrier, 15 + lax.div(6 - zh, 4) + lax.div(zh + 3, 4))

    def up_rows(q):
        return e_ref.at[pl.ds(UP_ROWS[q], PART)]

    def down_rows(q):
        return y_ref.at[pl.ds(SPAN + q * PART, PART)]

    def slot(buf, q):
        return buf.at[pl.ds(pl.multiple_of(q * PART, PART), PART)]

    up_far = [
        send(up_rows(q), relay_up, up_s.at[q], relay_r.at[0], at_y(q)) for q in range(3)
    ] + [send(up_rows(3), slot(eprev, 3), up_s.at[3], up_r.at[3], above)]
    down_far = [send(down_rows(0), slot(ynext, 0), down_s.at[0], down_r.at[0], below)] + [
        send(down_rows(q), relay_down, down_s.at[q], relay_r.at[1], at_y(q))
        for q in range(1, 4)
    ]
    up_near = [
        send(up_rows(q), slot(eprev, q), up_s.at[q], up_r.at[q], (d, p + 1)) for q in range(4)
    ]
    down_near = [
        send(down_rows(q), slot(ynext, q), down_s.at[q], down_r.at[q], (d, p - 1))
        for q in range(4)
    ]
    pass_up = send(relay_up, slot(eprev, y), relay_s.at[0], up_r.at[y], above)
    pass_down = send(relay_down, slot(ynext, y), relay_s.at[1], down_r.at[y], below)
    up_is_far, down_is_far = (y == 3) & rises, (y == 0) & falls
    relays_up, relays_down = (y < 3) & rises, (y > 0) & falls

    @pl.when(up_is_far)
    def _():
        for copy in up_far:
            copy.start()

    @pl.when(down_is_far)
    def _():
        for copy in down_far:
            copy.start()

    halo_copies = [
        send(e_ref.at[pl.ds(3 * SPAN, SPAN)], halo.at[0], halo_s.at[0], halo_r.at[0], (after, p)),
        send(e_ref.at[pl.ds(0, SPAN)], halo.at[1], halo_s.at[1], halo_r.at[1], (before, p)),
    ]
    for copy in halo_copies:
        copy.start()
    freq_copy = send(freq_mine, freq_next, freq_sem.at[0], freq_sem.at[1], (d, p - 1))

    @pl.when(has_prev)
    def _():
        freq_copy.start()

    @pl.when(relays_up)
    def _():
        pass_up_in = send(relay_up, relay_up, relay_s.at[0], relay_r.at[0], above)
        pass_up_in.wait_recv()
        pass_up.start()

    @pl.when(relays_down)
    def _():
        pass_down_in = send(relay_down, relay_down, relay_s.at[1], relay_r.at[1], below)
        pass_down_in.wait_recv()
        pass_down.start()

    @pl.when(y < 3)
    def _():
        for copy in up_near:
            copy.start()

    @pl.when(y > 0)
    def _():
        for copy in down_near:
            copy.start()

    for copy in halo_copies:
        copy.wait_recv()
    for g, side, away, near in ((0, 0, 0, 2), (3, 1, 5, 3)):
        total = mm(coupling(g, away), halo[side]) + mm(coupling(g, near), own_block(near - 1))
        y_ref[g * SPAN:(g + 1) * SPAN, :] = total.astype(BF16)

    def fill(m, lefts, rights):
        def tile(i, carry):
            cols = pl.ds(pl.multiple_of(i * 256, 256), 256)
            total = None
            for left, right in zip(lefts, rights):
                part = mtm(left[:, cols], right[...])
                total = part if total is None else total + part
            pairs[m, pl.ds(i * 16, 16)] = total.reshape(16, 2, 8, MODES)
            return carry

        lax.fori_loop(0, 2, tile, 0)

    def core_copy(m):
        return send(
            pairs.at[m, :, 1 - c], core_in.at[m], core_sem.at[0, m], core_sem.at[1, m],
            (d + 1 - 2 * c, p),
        )

    def x_copy(m, k):
        return send(
            x_out.at[m, k - 1], x_in.at[m, k - 1], x_s.at[m, k - 1], x_r.at[m, k - 1], at_x(k)
        )

    def z_copy(m, k):
        return send(
            z_out.at[m, lax.rem(zl + k, 8)], z_in.at[m, k - 1],
            z_s.at[m, k - 1], z_r.at[m, k - 1], at_z(k),
        )

    def after_core(m, xx):
        rows = pl.ds(pl.multiple_of(xx * 8, 8), 8)
        return pairs[m, rows, c] + core_in[m, rows]

    def start_x(m):
        core_copy(m).wait_recv()
        for k in (1, 2, 3):
            value = after_core(m, lax.rem(x + k, 4))
            x_out[m, k - 1] = value.reshape(64, MODES).astype(BF16)
            x_copy(m, k).start()

    def start_z(m):
        total = after_core(m, x)
        for k in (1, 2, 3):
            x_copy(m, k).wait_recv()
            total = total + x_in[m, k - 1].astype(F32).reshape(8, 8, MODES)
        z_out[m] = total
        for k in range(1, 8):
            z_copy(m, k).start()

    def finish(m):
        total = z_out[m, zl]
        for k in range(1, 8):
            z_copy(m, k).wait_recv()
            total = total + z_in[m, k - 1]
        return total

    fill(SELF, (e_ref,), (y_ref,))
    core_copy(SELF).start()
    start_x(SELF)
    start_z(SELF)

    def run_next():
        for q in range(4):
            up = send(slot(ynext, q), slot(ynext, q), down_s.at[q], down_r.at[q], (d, p + 1))
            up.wait_recv()
        fill(NEXT, (e_ref.at[pl.ds(SPAN, 2 * SPAN)],), (ynext,))
        core_copy(NEXT).start()
        start_x(NEXT)
        start_z(NEXT)

    prev_copy = send(prev_out, prev_in, prev_sem.at[0], prev_sem.at[1], (d, p - 1))

    def run_prev():
        for q in range(4):
            up = send(slot(eprev, q), slot(eprev, q), up_s.at[q], up_r.at[q], (d, p - 1))
            up.wait_recv()
        fill(
            PREV,
            (eprev.at[pl.ds(0, SPAN)], eprev.at[pl.ds(SPAN, SPAN)]),
            (y_ref.at[pl.ds(0, SPAN)], y_ref.at[pl.ds(3 * SPAN, SPAN)]),
        )
        core_copy(PREV).start()
        start_x(PREV)
        start_z(PREV)
        prev_out[...] = finish(PREV)
        prev_copy.start()

    @pl.when(y == 3)
    def _():
        run_prev()

    @pl.when(has_next)
    def _():
        run_next()

    @pl.when((y < 3) & has_prev)
    def _():
        run_prev()

    lane = lax.broadcasted_iota(jnp.int32, (8, MODES), 1)
    row = lax.broadcasted_iota(jnp.int32, (8, MODES), 0)

    def window(which):
        tiles = [mask_ref[which, x, j].astype(F32) for j in range(4)]
        return jnp.where(
            lane < 256,
            jnp.where(lane < 128, tiles[0], tiles[1]),
            jnp.where(lane < 384, tiles[2], tiles[3]),
        )

    w_all = freq_mine[...]
    w_mine = jnp.sum(jnp.where(lane == 8 * d + row, w_all, 0.0), axis=1, keepdims=True)
    own_pairs = finish(SELF) * window(0)
    self_ref[0] = own_pairs
    total = jnp.sum(own_pairs * own_pairs * lorentz(w_mine - w_all), axis=1, keepdims=True)
    scale = math.pi / 3.0 / (2.0 * MODES * w_mine * w_mine)
    lane8 = lax.broadcasted_iota(jnp.int32, (8, 128), 1)
    row8 = lax.broadcasted_iota(jnp.int32, (8, 128), 0)

    def put(sums):
        spread = jnp.where(lane8 == row8, sums * scale, 0.0)
        diff_ref[...] = jnp.sum(spread, axis=0, keepdims=True)[:, 0:8]

    @pl.when(has_next)
    def _():
        send(freq_mine, freq_next, freq_sem.at[0], freq_sem.at[1], (d, p + 1)).wait_recv()
        send(prev_out, prev_in, prev_sem.at[0], prev_sem.at[1], (d, p + 1)).wait_recv()
        next_pairs = (finish(NEXT) + prev_in[...]) * window(1)
        next_ref[0] = next_pairs
        ahead = next_pairs * next_pairs * lorentz(w_mine - freq_next[...])
        put(total + jnp.sum(ahead, axis=1, keepdims=True))

    @pl.when(p == 15)
    def _():
        next_ref[0] = jnp.zeros((8, MODES), F32)
        put(total)

    @pl.when(has_next)
    def _():
        for q in range(4):
            up_near[q].wait_send()

    @pl.when(has_prev)
    def _():
        for q in range(4):
            down_near[q].wait_send()
        freq_copy.wait_send()
        prev_copy.wait_send()

    for copy in halo_copies:
        copy.wait_send()

    @pl.when(relays_up)
    def _():
        pass_up.wait_send()

    @pl.when(relays_down)
    def _():
        pass_down.wait_send()

    def drain(m):
        core_copy(m).wait_send()
        for k in (1, 2, 3):
            x_copy(m, k).wait_send()
        for k in range(1, 8):
            z_copy(m, k).wait_send()

    drain(SELF)

    @pl.when(has_next)
    def _():
        drain(NEXT)

    @pl.when(has_prev)
    def _():
        drain(PREV)


def shards(eigvec, flux, blocks, tile_mask, freq):
    vmem = pl.BlockSpec(memory_space=pltpu.VMEM)
    smem = pl.BlockSpec(memory_space=pltpu.SMEM)
    dma = pltpu.SemaphoreType.DMA
    return pl.pallas_call(
        kernel,
        out_shape=(
            jax.ShapeDtypeStruct((1, 8, MODES), F32),
            jax.ShapeDtypeStruct((1, 8, MODES), F32),
            jax.ShapeDtypeStruct((1, 8), F32),
        ),
        in_specs=[vmem, vmem, smem, smem, vmem],
        out_specs=(vmem, vmem, vmem),
        scratch_shapes=[
            pltpu.VMEM((4 * SPAN, MODES), BF16),
            pltpu.VMEM((2, SPAN, MODES), BF16),
            pltpu.VMEM((2 * SPAN, MODES), BF16),
            pltpu.VMEM((2 * SPAN, MODES), BF16),
            pltpu.VMEM((PART, MODES), BF16),
            pltpu.VMEM((PART, MODES), BF16),
            pltpu.VMEM((8, MODES), F32),
            pltpu.VMEM((8, MODES), F32),
            pltpu.VMEM((3, 32, 2, 8, MODES), F32),
            pltpu.VMEM((3, 32, 8, MODES), F32),
            pltpu.VMEM((3, 3, 64, MODES), BF16),
            pltpu.VMEM((3, 3, 64, MODES), BF16),
            pltpu.VMEM((3, 8, 8, MODES), F32),
            pltpu.VMEM((3, 7, 8, MODES), F32),
            pltpu.VMEM((8, MODES), F32),
            pltpu.VMEM((8, MODES), F32),
            dma((2,)), dma((2,)),
            dma((4,)), dma((4,)),
            dma((4,)), dma((4,)),
            dma((2,)), dma((2,)),
            dma((2,)),
            dma((2, 3)),
            dma((3, 3)), dma((3, 3)),
            dma((3, 7)), dma((3, 7)),
            dma((2,)),
        ],
        compiler_params=pltpu.CompilerParams(
            collective_id=0, has_side_effects=True, vmem_limit_bytes=48 << 20
        ),
        cost_estimate=pl.CostEstimate(
            flops=3_000_000_000, bytes_accessed=4_000_000, transcendentals=0
        ),
    )(eigvec, flux, blocks, tile_mask[0], freq)


def solution(mesh):
    return jax.shard_map(
        shards,
        mesh=mesh,
        in_specs=(
            P("domain", "panel"),
            P("domain", None),
            P("domain", None),
            P("panel", None, None, None),
            P("panel", None),
        ),
        out_specs=(P("panel", "domain", None), P("panel", "domain", None), P("panel", "domain")),
        check_vma=False,
    )
```

time: 800 us -> 115 us (0.14)
  waiting for transfers between devices: 736 us -> 0 us
  Pallas kernels: 0 us -> 107 us
  starting transfers between devices: 21.3 us -> 0 us
  between operations: 14.2 us -> 0.64 us
  other arithmetic: 8.68 us -> 0 us
    reduce_scatter x1 -> x0, waiting for transfers between devices: 451 us -> none  [shards(): lax.psum_scatter(contract(eigvec, joined), 'domain', scatter_dimension=0,...]
    ppermute x4 -> x0, waiting for transfers between devices: 284 us -> none  [the longest x2 281 us: shifted(): lax.ppermute(value, axis, [(source, source + steps) for source in range(i...]
    pallas_call x0 -> x1, Pallas kernels: none -> 107 us  [shards(): pl.pallas_call(kernel, out_shape=(jax.ShapeDtypeStruct((1, 8, MODES), F32...]
    ppermute x4 -> x0, starting transfers between devices: 21.3 us -> none  [the longest x1 14.8 us: padded(): lax.ppermute(head, axis, [((i + 1) % count, i) for i in range(count)])]
  transfers between devices with their start and end apart: 5 -> 0, of which waited for: 5 -> 0; matrix products, arithmetic and copies ran while one was open for 1% -> 0% of each run, Pallas kernels for 0% -> 0%
where the time goes in v1:
time: 115 us
  Pallas kernels  107 us (93%)
  local copies, waits for them, and re-layouts  6.93 us (6%)
    pallas_call x1, Pallas kernels, shards(): pl.pallas_call(kernel, out_shape=(jax.ShapeDtypeStruct((1, 8, MODES), F32...  107 us
    unnamed x12, local copies, waits for them, and re-layouts  6.93 us

profile of v1, /device:TPU:24, one launch (start us, length us, event | category | flops | bytes accessed | tf_op | source)
XLA Modules:
  0.0 114.6 jit_solution(6367186501590017579)
XLA Ops:
  0.6 0.8 copy.8.blocks_ref
  1.4 0.0 copy-start
  1.4 1.7 %copy-done = bf16[1536,768]{1,0:T(8,128)(2,1)S(1)} copy-done((bf16[1536,768]{1,0:T(8,128)(2,1)S(1)}, bf16[1536,768]{1,0:T(8,128)(2,1)}, u32[]{:S(2)}) %copy-start) | copy-done | bytes 2359320
  3.1 0.0 copy-start.1
  3.1 1.4 %copy-done.1 = bf16[1536,512]{1,0:T(8,128)(2,1)S(1)} copy-done((bf16[1536,512]{1,0:T(8,128)(2,1)S(1)}, bf16[1536,512]{1,0:T(8,128)(2,1)}, u32[]{:S(2)}) %copy-start.1) | copy-done | bytes 1572888
  4.5 0.0 copy-start.2
  4.5 0.7 copy-done.2
  5.2 0.0 copy-start.3
  5.2 0.7 copy-done.3
  5.8 107.0 %shard_map.76 = (f32[1,8,512]{2,1,0:T(8,128)S(1)}, f32[1,8,512]{2,1,0:T(8,128)S(1)}, f32[1,8]{1,0:T(1,128)S(1)}) custom-call(bf16[1536,512]{1,0:T(8,128)(2,1)S(1)} %copy-done.1, bf16[1536,768]{1,0:T(8,128)(2,1)S(1)} %copy-done, s32[4,2]{1,0:T(4,128)S(1)} %copy.8.blocks_ref, s32[2,4,4]{2,1,0:T(4,128)S(1)} %bitcast.1, bf16[1,512]{1,0:T(2,128)(2,1)S(1)} %copy-done.3), custom_call_target="tpu_custom_call" | custom-call | flops 3000000000 | bytes 4000000 | tf_op jit(solution)/shard_map/pallas_call | solution.py:374
  112.8 0.6 copy.12
  113.4 0.6 copy.13
  114.0 0.5 copy.14
Async XLA Ops:
  1.4 1.7 %copy-start = (bf16[1536,768]{1,0:T(8,128)(2,1)S(1)}, bf16[1536,768]{1,0:T(8,128)(2,1)}, u32[]{:S(2)}) copy-start(bf16[1536,768]{1,0:T(8,128)(2,1)} %f_ref.1) | copy-start | bytes 7077892
  3.1 1.4 %copy-start.1 = (bf16[1536,512]{1,0:T(8,128)(2,1)S(1)}, bf16[1536,512]{1,0:T(8,128)(2,1)}, u32[]{:S(2)}) copy-start(bf16[1536,512]{1,0:T(8,128)(2,1)} %e_ref.1) | copy-start | bytes 4718596
  4.5 0.7 copy-start.2
  5.2 0.7 copy-start.3

commit v2 on v1

v2 whole, which is shorter than its diff:
```python
import math

import jax
import jax.numpy as jnp
from jax import lax
from jax.experimental import pallas as pl
from jax.experimental.pallas import tpu as pltpu
from jax.sharding import PartitionSpec as P

MESH = pl.DeviceIdType.MESH
F32 = jnp.float32
BF16 = jnp.bfloat16

WIDTH = 0.25
SPAN = 384
MODES = 512
PART = 192
LANES = 128
SELF, NEAR, FAR = 0, 1, 2


def lorentz(gap):
    return WIDTH / math.pi / (gap * gap + WIDTH * WIDTH)


def mm(a, b):
    return jnp.dot(a, b, preferred_element_type=F32)


def mtm(a, b):
    return lax.dot_general(a, b, (((0,), (0,)), ((), ())), preferred_element_type=F32)


def chunk(k):
    return pl.ds(pl.multiple_of(k * LANES, LANES), LANES)


def kernel(
    e_in, f_in, blocks_in, mask_in, freq_in,
    self_ref, next_ref, diff_ref,
    e_ref, f_ref, blocks_ref, mask_ref, freq_ref,
    y_ref, halo, eprev, ynext, relay_up, relay_down, freq_mine, freq_next, next_sum,
    pairs, core_in, x_out, x_in, z_own, z_out, z_in, piece_out, piece_in,
    load_sem, halo_s, halo_r, up_s, up_r, down_s, down_r, relay_s, relay_r, freq_sem,
    core_s, core_r, x_s, x_r, z_s, z_r, piece_sem, ready,
):
    d = lax.axis_index("domain")
    p = lax.axis_index("panel")
    x, zl, c = d // 16, lax.rem(d // 2, 8), lax.rem(d, 2)
    y, zh = lax.rem(p, 4), p // 4
    has_next, has_prev = p < 15, p > 0
    rises, falls = zh < 3, zh > 0
    after, before = lax.rem(d + 1, 64), lax.rem(d + 63, 64)
    above, below = (d, zh * 4 + 4), (d, zh * 4 - 1)

    loads = [
        pltpu.make_async_copy(src, dst, load_sem.at[i])
        for i, (src, dst) in enumerate(
            ((e_in, e_ref), (f_in, f_ref), (blocks_in, blocks_ref), (freq_in, freq_ref), (mask_in, mask_ref))
        )
    ]
    for load in loads:
        load.start()

    def at_x(k):
        return (lax.rem(x + k, 4) * 16 + zl * 2 + c, p)

    def at_z(k):
        return (x * 16 + lax.rem(zl + k, 8) * 2 + c, p)

    def at_y(q):
        return (d, zh * 4 + q)

    def send(src, dst, send_sem, recv_sem, device):
        return pltpu.make_async_remote_copy(
            src_ref=src, dst_ref=dst, send_sem=send_sem, recv_sem=recv_sem,
            device_id=device, device_id_type=MESH,
        )

    barrier = pltpu.get_barrier_semaphore()

    def greet(device):
        pl.semaphore_signal(barrier, inc=1, device_id=device, device_id_type=MESH)

    @pl.when((y == 3) & rises)
    def _():
        for q in range(4):
            greet((d, zh * 4 + 4 + q))

    @pl.when((y < 3) & rises)
    def _():
        greet(above)

    for k in range(1, 8):
        greet(at_z(k))
    greet((after, p))
    greet((before, p))
    for k in (1, 2, 3):
        greet(at_y(lax.rem(y + k, 4)))
        greet(at_x(k))

    def coupling(g, entry):
        rows = slice(g * SPAN, (g + 1) * SPAN)
        total = None
        for k in range(2):
            listed = jnp.full((1, SPAN), blocks_ref[k, g], jnp.int32) == entry
            weight = jnp.where(listed, 1.0, 0.0).astype(BF16)
            part = f_ref[rows, k * SPAN:(k + 1) * SPAN] * weight
            total = part if total is None else total + part
        return total

    def own_block(b):
        return e_ref[b * SPAN:(b + 1) * SPAN, :]

    for load in loads:
        load.wait()
    for g in (1, 2):
        total = mm(coupling(g, g), own_block(g - 1))
        total += mm(coupling(g, g + 1), own_block(g))
        total += mm(coupling(g, g + 2), own_block(g + 1))
        y_ref[g * SPAN:(g + 1) * SPAN, :] = total.astype(BF16)

    freq_mine[...] = jnp.broadcast_to(freq_ref[...].astype(F32), (8, MODES))

    from_below = lax.div(zh + 3, 4) * (1 + 3 * lax.div(3 - y, 3))
    pl.semaphore_wait(barrier, 15 + from_below)

    @pl.when((y == 0) & falls)
    def _():
        for q in range(4):
            pl.semaphore_signal(
                ready, inc=1, device_id=(d, zh * 4 - 4 + q), device_id_type=MESH
            )

    def quarter(buf, q, k):
        return buf.at[pl.ds(pl.multiple_of(q * PART, PART), PART), chunk(k)]

    def up_part(q, k):
        start = q * PART + lax.div(q, 2) * (2 * SPAN)
        return e_ref.at[pl.ds(pl.multiple_of(start, PART), PART), chunk(k)]

    def down_part(q, k):
        return y_ref.at[pl.ds(pl.multiple_of(SPAN + q * PART, PART), PART), chunk(k)]

    def up(q, k, device):
        return send(up_part(q, k), quarter(eprev, q, k), up_s.at[q, k], up_r.at[q, k], device)

    def down(q, k, device):
        return send(
            down_part(q, k), quarter(ynext, q, k), down_s.at[q, k], down_r.at[q, k], device
        )

    def to_relay_up(q, k):
        return send(
            up_part(q, k), relay_up.at[:, chunk(k)], up_s.at[q, k], relay_r.at[0, k], at_y(q)
        )

    def to_relay_down(q, k):
        return send(
            down_part(q, k), relay_down.at[:, chunk(k)], down_s.at[q, k], relay_r.at[1, k], at_y(q)
        )

    def pass_up(k):
        return send(
            relay_up.at[:, chunk(k)], quarter(eprev, y, k), relay_s.at[0, k], up_r.at[y, k], above
        )

    def pass_down(k):
        return send(
            relay_down.at[:, chunk(k)], quarter(ynext, y, k),
            relay_s.at[1, k], down_r.at[y, k], below,
        )

    halo_copies = [
        send(e_ref.at[pl.ds(3 * SPAN, SPAN)], halo.at[0], halo_s.at[0], halo_r.at[0], (after, p)),
        send(e_ref.at[pl.ds(0, SPAN)], halo.at[1], halo_s.at[1], halo_r.at[1], (before, p)),
    ]
    for copy in halo_copies:
        copy.start()

    @pl.when((y == 3) & rises)
    def _():
        @pl.loop(0, 4)
        def _(k):
            for q in (2, 0, 1):
                to_relay_up(q, k).start()

    @pl.when((y == 0) & falls)
    def _():
        @pl.loop(0, 4)
        def _(k):
            for q in (1, 3, 2):
                to_relay_down(q, k).start()

    freq_copy = send(freq_mine, freq_next, freq_sem.at[0], freq_sem.at[1], (d, p - 1))

    @pl.when(has_prev)
    def _():
        freq_copy.start()

    relays_up, relays_down = (y < 3) & rises, (y > 0) & falls

    @pl.loop(0, 4)
    def _(k):
        @pl.when(y < 3)
        def _():
            for q in range(4):
                up(q, k, (d, p + 1)).start()

        @pl.when(y > 0)
        def _():
            for q in range(4):
                down(q, k, (d, p - 1)).start()

    def cross_up():
        @pl.when(rises)
        def _():
            pl.semaphore_wait(ready, 1)

        @pl.when((y == 3) & rises)
        def _():
            @pl.loop(0, 4)
            def _(k):
                up(3, k, above).start()

        @pl.when(relays_up)
        def _():
            @pl.loop(0, 4)
            def _(k):
                send(
                    relay_up.at[:, chunk(k)], relay_up.at[:, chunk(k)],
                    relay_s.at[0, k], relay_r.at[0, k], above,
                ).wait_recv()
                pass_up(k).start()

    def cross_down():
        @pl.when((y == 0) & falls)
        def _():
            @pl.loop(0, 4)
            def _(k):
                down(0, k, below).start()

        @pl.when(relays_down)
        def _():
            @pl.loop(0, 4)
            def _(k):
                send(
                    relay_down.at[:, chunk(k)], relay_down.at[:, chunk(k)],
                    relay_s.at[1, k], relay_r.at[1, k], below,
                ).wait_recv()
                pass_down(k).start()

    for copy in halo_copies:
        copy.wait_recv()

    pl.when(zl < 4)(cross_up)
    pl.when(zl >= 4)(cross_down)

    for g, side, away, near in ((0, 0, 0, 2), (3, 1, 5, 3)):
        total = mm(coupling(g, away), halo[side]) + mm(coupling(g, near), own_block(near - 1))
        y_ref[g * SPAN:(g + 1) * SPAN, :] = total.astype(BF16)

    other_core = (d + 1 - 2 * c, p)

    def fill(m, lefts, rights):
        @pl.loop(0, 2)
        def _(i):
            cols = pl.ds(pl.multiple_of(i * 256, 256), 256)
            total = None
            for left, right in zip(lefts, rights):
                part = mtm(left[:, cols], right[...])
                total = part if total is None else total + part
            pairs[m, pl.ds(i * 16, 16)] = total.reshape(16, 2, 8, MODES)

    def core_copy(m):
        return send(
            pairs.at[m, :, 1 - c], core_in.at[m], core_s.at[m], core_r.at[m], other_core
        )

    def x_copy(m, k):
        return send(
            x_out.at[m, k - 1], x_in.at[m, k - 1], x_s.at[m, k - 1], x_r.at[m, k - 1], at_x(k)
        )

    def z_copy(m, k):
        return send(
            z_out.at[m, lax.rem(zl + k, 8)], z_in.at[m, k - 1],
            z_s.at[m, k - 1], z_r.at[m, k - 1], at_z(k),
        )

    def after_core(m, xx):
        rows = pl.ds(pl.multiple_of(xx * 8, 8), 8)
        return pairs[m, rows, c] + core_in[m, rows]

    def start_x(m):
        core_copy(m).wait_recv()
        for k in (1, 2, 3):
            value = after_core(m, lax.rem(x + k, 4))
            x_out[m, k - 1] = value.reshape(64, MODES).astype(BF16)
            x_copy(m, k).start()

    def start_z(m):
        total = after_core(m, x)
        for k in (1, 2, 3):
            x_copy(m, k).wait_recv()
            total = total + x_in[m, k - 1].astype(F32).reshape(8, 8, MODES)
        z_own[m] = total
        halves = jnp.concatenate([total[:, :, :256], total[:, :, 256:]], axis=1)
        z_out[m] = halves.astype(BF16)
        for k in range(1, 8):
            z_copy(m, k).start()

    def finish(m):
        for k in range(1, 8):
            z_copy(m, k).wait_recv()
        arrived = z_in[m, 0].astype(F32)
        for k in range(2, 8):
            arrived = arrived + z_in[m, k - 1].astype(F32)
        return z_own[m, zl] + jnp.concatenate([arrived[:8], arrived[8:]], axis=1)

    def await_up(k):
        for q in range(4):
            send(
                quarter(eprev, q, k), quarter(eprev, q, k), up_s.at[q, k], up_r.at[q, k], (d, p - 1)
            ).wait_recv()

    def await_down(k):
        for q in range(4):
            send(
                quarter(ynext, q, k), quarter(ynext, q, k),
                down_s.at[q, k], down_r.at[q, k], (d, p + 1),
            ).wait_recv()

    inner_e = e_ref.at[pl.ds(SPAN, 2 * SPAN)]
    prev_pair = (
        (eprev.at[pl.ds(0, SPAN)], eprev.at[pl.ds(SPAN, SPAN)]),
        (y_ref.at[pl.ds(0, SPAN)], y_ref.at[pl.ds(3 * SPAN, SPAN)]),
    )
    def piece_copy(device):
        return send(piece_out, piece_in, piece_sem.at[0], piece_sem.at[1], device)

    def next_part():
        for k in range(4):
            await_down(k)
        return (inner_e,), (ynext,)

    def prev_part():
        for k in range(4):
            await_up(k)
        return prev_pair

    fill(SELF, (e_ref,), (y_ref,))
    core_copy(SELF).start()
    start_x(SELF)
    start_z(SELF)
    pl.when(zl >= 4)(cross_up)
    pl.when(zl < 4)(cross_down)

    @pl.when(y == 3)
    def _():
        fill(NEAR, *prev_part())

    @pl.when(y < 3)
    def _():
        fill(NEAR, *next_part())

    core_copy(NEAR).start()
    start_x(NEAR)
    start_z(NEAR)
    has_far = jnp.logical_or((y == 3) & rises, (y < 3) & has_prev)

    @pl.when((y == 3) & rises)
    def _():
        fill(FAR, *next_part())

    @pl.when((y < 3) & has_prev)
    def _():
        fill(FAR, *prev_part())

    @pl.when(has_far)
    def _():
        core_copy(FAR).start()
        start_x(FAR)
        start_z(FAR)

    @pl.when((y == 3) & rises)
    def _():
        next_sum[...] = finish(FAR)

    @pl.when((y < 3) & has_prev)
    def _():
        piece_out[...] = finish(FAR)
        piece_copy((d, p - 1)).start()

    near = finish(NEAR)

    @pl.when(y == 3)
    def _():
        piece_out[...] = near
        piece_copy((d, p - 1)).start()

    @pl.when(y < 3)
    def _():
        next_sum[...] = near

    lane = lax.broadcasted_iota(jnp.int32, (8, MODES), 1)
    row = lax.broadcasted_iota(jnp.int32, (8, MODES), 0)

    def window(which):
        tiles = [mask_ref[0, which, x, j].astype(F32) for j in range(4)]
        return jnp.where(
            lane < 256,
            jnp.where(lane < 128, tiles[0], tiles[1]),
            jnp.where(lane < 384, tiles[2], tiles[3]),
        )

    w_all = freq_mine[...]
    w_mine = jnp.sum(jnp.where(lane == 8 * d + row, w_all, 0.0), axis=1, keepdims=True)
    own_pairs = finish(SELF) * window(0)
    self_ref[0] = own_pairs
    total = jnp.sum(own_pairs * own_pairs * lorentz(w_mine - w_all), axis=1, keepdims=True)
    scale = math.pi / 3.0 / (2.0 * MODES * w_mine * w_mine)
    lane8 = lax.broadcasted_iota(jnp.int32, (8, 128), 1)
    row8 = lax.broadcasted_iota(jnp.int32, (8, 128), 0)

    def put(sums):
        spread = jnp.where(lane8 == row8, sums * scale, 0.0)
        diff_ref[...] = jnp.sum(spread, axis=0, keepdims=True)[:, 0:8]

    @pl.when(has_next)
    def _():
        send(freq_mine, freq_next, freq_sem.at[0], freq_sem.at[1], (d, p + 1)).wait_recv()
        weights = lorentz(w_mine - freq_next[...])
        piece_copy((d, p + 1)).wait_recv()
        next_pairs = (next_sum[...] + piece_in[...]) * window(1)
        next_ref[0] = next_pairs
        put(total + jnp.sum(next_pairs * next_pairs * weights, axis=1, keepdims=True))

    @pl.when(p == 15)
    def _():
        next_ref[0] = jnp.zeros((8, MODES), F32)
        put(total)

    @pl.loop(0, 4)
    def _(k):
        @pl.when(has_next)
        def _():
            for q in range(4):
                up(q, k, above).wait_send()

        @pl.when(has_prev)
        def _():
            for q in range(4):
                down(q, k, below).wait_send()

        @pl.when(relays_up)
        def _():
            pass_up(k).wait_send()

        @pl.when(relays_down)
        def _():
            pass_down(k).wait_send()

    @pl.when(has_prev)
    def _():
        freq_copy.wait_send()
        piece_copy((d, p - 1)).wait_send()

    for copy in halo_copies:
        copy.wait_send()

    def drain(m):
        core_copy(m).wait_send()
        for k in (1, 2, 3):
            x_copy(m, k).wait_send()
        for k in range(1, 8):
            z_copy(m, k).wait_send()

    drain(SELF)
    drain(NEAR)

    @pl.when(has_far)
    def _():
        drain(FAR)


def hand_out(a_ref, b_ref, c_ref, self_ref, next_ref, diff_ref):
    self_ref[...] = a_ref[...]
    next_ref[...] = b_ref[...]
    diff_ref[...] = c_ref[...]


def shards(eigvec, flux, blocks, tile_mask, freq):
    vmem = pl.BlockSpec(memory_space=pltpu.VMEM)
    hbm = pl.BlockSpec(memory_space=pltpu.MemorySpace.HBM)
    dma = pltpu.SemaphoreType.DMA
    sums = pl.pallas_call(
        kernel,
        out_shape=(
            jax.ShapeDtypeStruct((1, 8, MODES), F32),
            jax.ShapeDtypeStruct((1, 8, MODES), F32),
            jax.ShapeDtypeStruct((1, 8), F32),
        ),
        in_specs=[hbm] * 5,
        out_specs=(vmem, vmem, vmem),
        scratch_shapes=[
            pltpu.VMEM((4 * SPAN, MODES), BF16),
            pltpu.VMEM((4 * SPAN, 2 * SPAN), BF16),
            pltpu.SMEM((2, 4), jnp.int32),
            pltpu.SMEM((1, 2, 4, 4), jnp.int32),
            pltpu.VMEM((1, MODES), BF16),
            pltpu.VMEM((4 * SPAN, MODES), BF16),
            pltpu.VMEM((2, SPAN, MODES), BF16),
            pltpu.VMEM((2 * SPAN, MODES), BF16),
            pltpu.VMEM((2 * SPAN, MODES), BF16),
            pltpu.VMEM((PART, MODES), BF16),
            pltpu.VMEM((PART, MODES), BF16),
            pltpu.VMEM((8, MODES), F32),
            pltpu.VMEM((8, MODES), F32),
            pltpu.VMEM((8, MODES), F32),
            pltpu.VMEM((3, 32, 2, 8, MODES), F32),
            pltpu.VMEM((3, 32, 8, MODES), F32),
            pltpu.VMEM((3, 3, 64, MODES), BF16),
            pltpu.VMEM((3, 3, 64, MODES), BF16),
            pltpu.VMEM((3, 8, 8, MODES), F32),
            pltpu.VMEM((3, 8, 16, 256), BF16),
            pltpu.VMEM((3, 7, 16, 256), BF16),
            pltpu.VMEM((8, MODES), F32),
            pltpu.VMEM((8, MODES), F32),
            dma((5,)),
            dma((2,)), dma((2,)),
            dma((4, 4)), dma((4, 4)),
            dma((4, 4)), dma((4, 4)),
            dma((2, 4)), dma((2, 4)),
            dma((2,)),
            dma((3,)), dma((3,)),
            dma((3, 3)), dma((3, 3)),
            dma((3, 7)), dma((3, 7)),
            dma((2,)),
            pltpu.SemaphoreType.REGULAR,
        ],
        compiler_params=pltpu.CompilerParams(
            collective_id=0, has_side_effects=True, vmem_limit_bytes=62 << 20
        ),
        cost_estimate=pl.CostEstimate(
            flops=3_000_000_000, bytes_accessed=4_000_000, transcendentals=0
        ),
    )(eigvec, flux, blocks.T, tile_mask, freq)
    return pl.pallas_call(
        hand_out,
        out_shape=tuple(jax.ShapeDtypeStruct(v.shape, v.dtype) for v in sums),
        in_specs=[vmem] * 3,
        out_specs=(vmem, vmem, vmem),
    )(*sums)


def solution(mesh):
    return jax.shard_map(
        shards,
        mesh=mesh,
        in_specs=(
            P("domain", "panel"),
            P("domain", None),
            P("domain", None),
            P("panel", None, None, None),
            P("panel", None),
        ),
        out_specs=(P("panel", "domain", None), P("panel", "domain", None), P("panel", "domain")),
        check_vma=False,
    )
```

time: 115 us -> 102 us (0.89)
  local copies, waits for them, and re-layouts: 6.93 us -> 0 us
  Pallas kernels: 107 us -> 101 us
    pallas_call x1, Pallas kernels: 107 us -> 99.8 us  [shards(): pl.pallas_call(kernel, out_shape=(jax.ShapeDtypeStruct((1, 8, MODES), F32...]
    unnamed x12 -> x0, local copies, waits for them, and re-layouts: 6.93 us -> none
    pallas_call x0 -> x1, Pallas kernels: none -> 1.35 us  [shards(): pl.pallas_call(hand_out, out_shape=tuple((jax.ShapeDtypeStruct(v.shape, v...]
where the time goes in v2:
time: 102 us
  Pallas kernels  101 us (99%)
    pallas_call x1, Pallas kernels, shards(): pl.pallas_call(kernel, out_shape=(jax.ShapeDtypeStruct((1, 8, MODES), F32...  99.8 us

profile of v2, /device:TPU:24, one launch (start us, length us, event | category | flops | bytes accessed | tf_op | source)
XLA Modules:
  0.0 101.8 jit_solution(1839527023889842647)
XLA Ops:
  0.6 99.8 %shard_map.76 = (f32[1,8,512]{2,1,0:T(8,128)}, f32[1,8,512]{2,1,0:T(8,128)}, f32[1,8]{1,0:T(1,128)}) custom-call(bf16[1536,512]{1,0:T(8,128)(2,1)} %e_in.1, bf16[1536,768]{1,0:T(8,128)(2,1)} %f_in.1, s32[2,4]{1,0:T(2,128)} %bitcast.1, s32[1,2,4,4]{3,2,1,0:T(4,128)} %mask_in.1, bf16[1,512]{1,0:T(2,128)(2,1)} %freq_in.1), custom_call_target="tpu_custom_call" | custom-call | flops 3000000000 | bytes 4000000 | tf_op jit(solution)/shard_map/pallas_call | solution.py:497
  100.4 1.4 %shard_map.77 = (f32[1,8,512]{2,1,0:T(8,128)}, f32[1,8,512]{2,1,0:T(8,128)}, f32[1,8]{1,0:T(1,128)}) custom-call(f32[1,8,512]{2,1,0:T(8,128)} %get-tuple-element.6.a_ref, f32[1,8,512]{2,1,0:T(8,128)} %get-tuple-element.7.b_ref, f32[1,8]{1,0:T(1,128)} %get-tuple-element.8.c_ref), custom_call_target="tpu_custom_call" | custom-call | tf_op jit(solution)/shard_map/pallas_call | solution.py:549

commit v3 on v2

--- a/solution.py
+++ b/solution.py
@@ -250,11 +250,13 @@
                 ).wait_recv()
                 pass_down(k).start()
 
+    pl.when(zh == 0)(cross_up)
+    pl.when((zh == 1) & (zl >= 4))(cross_down)
     for copy in halo_copies:
         copy.wait_recv()
 
-    pl.when(zl < 4)(cross_up)
-    pl.when(zl >= 4)(cross_down)
+    pl.when((zh > 0) & (zl < 4))(cross_up)
+    pl.when((zh > 1) & (zl >= 4))(cross_down)
 
     for g, side, away, near in ((0, 0, 0, 2), (3, 1, 5, 3)):
         total = mm(coupling(g, away), halo[side]) + mm(coupling(g, near), own_block(near - 1))
@@ -351,10 +353,11 @@
 
     fill(SELF, (e_ref,), (y_ref,))
     core_copy(SELF).start()
+    pl.when((zh == 1) & (zl < 4))(cross_down)
     start_x(SELF)
+    pl.when((zh > 0) & (zl >= 4))(cross_up)
+    pl.when((zh > 1) & (zl < 4))(cross_down)
     start_z(SELF)
-    pl.when(zl >= 4)(cross_up)
-    pl.when(zl < 4)(cross_down)
 
     @pl.when(y == 3)
     def _():

time: 102 us -> 99 us (0.971)
  Pallas kernels: 101 us -> 98.2 us
    pallas_call x1, Pallas kernels: 99.8 us -> 96.8 us  [shards(): pl.pallas_call(kernel, out_shape=(jax.ShapeDtypeStruct((1, 8, MODES), F32...]
where the time goes in v3:
time: 99 us; the launch traced here: 98.8 us
  Pallas kernels  98.2 us (99%)
    pallas_call x1, Pallas kernels, shards(): pl.pallas_call(kernel, out_shape=(jax.ShapeDtypeStruct((1, 8, MODES), F32...  96.8 us

profile of v3, /device:TPU:24, one launch (start us, length us, event | category | flops | bytes accessed | tf_op | source)
XLA Modules:
  0.0 98.8 jit_solution(2778702701967414432)
XLA Ops:
  0.6 96.8 %shard_map.76 = (f32[1,8,512]{2,1,0:T(8,128)}, f32[1,8,512]{2,1,0:T(8,128)}, f32[1,8]{1,0:T(1,128)}) custom-call(bf16[1536,512]{1,0:T(8,128)(2,1)} %e_in.1, bf16[1536,768]{1,0:T(8,128)(2,1)} %f_in.1, s32[2,4]{1,0:T(2,128)} %bitcast.1, s32[1,2,4,4]{3,2,1,0:T(4,128)} %mask_in.1, bf16[1,512]{1,0:T(2,128)(2,1)} %freq_in.1), custom_call_target="tpu_custom_call" | custom-call | flops 3000000000 | bytes 4000000 | tf_op jit(solution)/shard_map/pallas_call | solution.py:500
  97.4 1.4 %shard_map.77 = (f32[1,8,512]{2,1,0:T(8,128)}, f32[1,8,512]{2,1,0:T(8,128)}, f32[1,8]{1,0:T(1,128)}) custom-call(f32[1,8,512]{2,1,0:T(8,128)} %get-tuple-element.6.a_ref, f32[1,8,512]{2,1,0:T(8,128)} %get-tuple-element.7.b_ref, f32[1,8]{1,0:T(1,128)} %get-tuple-element.8.c_ref), custom_call_target="tpu_custom_call" | custom-call | tf_op jit(solution)/shard_map/pallas_call | solution.py:552
